TPU v7x, 32 devices: a whole 2x2x4 slice. The times are simulated.
32 devices in a mesh: wide: 16 (over z, x, core), narrow: 2 (over y).
Axes of the slice: x: 2, y: 2, z: 4, core: 2. Of those that a mesh axis runs over, the one named last changes fastest.
Arguments:
- krylov: float32 [2, 16777216], P(None, ('wide', 'narrow')), may hold values from -6 to 6
- fitness_class: int32 [524288], P(('wide', 'narrow')), may hold values from 0 to 7
- rate_index: int32 [2], replicated, may hold values from 4 to 15
Outputs:
- images: float32 [2, 16777216], P(None, ('wide', 'narrow'))
All inputs are finite; a program needn't handle non-finite values.
Results may differ from a plain program's by a relative error of at most 0.00014.
Values sent between devices are 32-bit elements; how exact they have to be, the bound alone decides.
A program may use at most 128 MiB of HBM per device.

v0:
```python
import jax
import jax.numpy as jnp
from jax import lax
from jax.sharding import PartitionSpec as P

ITERS = 2


def mutation_rates(rate_index, total_bits):
    levels = 0.004 * (rate_index.astype(jnp.float32) + 1.0)
    position = jnp.arange(total_bits, dtype=jnp.float32)
    profile = 1.0 + 0.5 * jnp.cos(2.0 * position)
    return levels[:, None] * profile[None, :]


def kronecker(mutation, first_site, width_bits):
    middle = 1 << width_bits
    indices = jnp.arange(middle, dtype=jnp.int32)
    product = jnp.ones((mutation.shape[0], middle, middle), jnp.float32)
    for bit_pos in range(width_bits):
        column = indices >> bit_pos & 1
        agreeing = column[:, None] == column[None, :]
        chance = mutation[:, first_site + bit_pos][:, None, None]
        product = product * jnp.where(agreeing[None], 1.0 - chance, chance)
    return product


def split_widths(amount):
    groups = -(-amount // 7)
    common = amount // groups
    leftover = amount % groups
    return [common + 1 if number < leftover else common for number in range(groups)]


def mix_range(vectors, mutation, first_pos, amount, site_shift):
    vector_count, length = vectors.shape
    offset = first_pos
    for group_width in split_widths(amount):
        low_size = 1 << offset
        middle = 1 << group_width
        high_size = length // (low_size * middle)
        matrix = kronecker(mutation, offset + site_shift, group_width)
        if low_size == 1:
            shaped = vectors.reshape(vector_count, high_size, middle)
            mixed_out = jnp.einsum("aij,ahj->ahi", matrix, shaped, precision=lax.Precision.HIGHEST)
        else:
            shaped = vectors.reshape(vector_count, high_size, middle, low_size)
            mixed_out = jnp.einsum(
                "aij,ahjl->ahil", matrix, shaped, precision=lax.Precision.HIGHEST
            )
        vectors = mixed_out.reshape(vector_count, length)
        offset = offset + group_width
    return vectors


def apply_fitness(vectors, classes):
    vector_count, length = vectors.shape
    blocks = classes.shape[0]
    scale_row = 0.5 + 0.25 * classes.astype(jnp.float32)
    shaped = vectors.reshape(vector_count, blocks, length // blocks) * scale_row[None, :, None]
    return shaped.reshape(vector_count, length)


def device_shape(vectors):
    vector_count, length = vectors.shape
    wide_count = lax.axis_size("wide")
    narrow_count = lax.axis_size("narrow")
    return vectors.reshape(
        vector_count, wide_count, narrow_count, length // (wide_count * narrow_count)
    )


def later_move(vectors):
    moved = lax.all_to_all(
        lax.all_to_all(device_shape(vectors), "wide", split_axis=1, concat_axis=1, tiled=True),
        "narrow",
        split_axis=2,
        concat_axis=2,
        tiled=True,
    )
    return moved.reshape(vectors.shape)


def first_move(vectors, classes):
    wide_count = lax.axis_size("wide")
    narrow_count = lax.axis_size("narrow")
    class_shaped = classes.reshape(
        1, wide_count, narrow_count, classes.shape[0] // (wide_count * narrow_count)
    )
    moved, moved_classes = (
        lax.all_to_all(
            lax.all_to_all(device_shape(vectors), "wide", split_axis=1, concat_axis=1, tiled=True),
            "narrow",
            split_axis=2,
            concat_axis=2,
            tiled=True,
        ),
        lax.all_to_all(
            lax.all_to_all(class_shaped, "wide", split_axis=1, concat_axis=1, tiled=True),
            "narrow",
            split_axis=2,
            concat_axis=2,
            tiled=True,
        ),
    )
    return (moved.reshape(vectors.shape), moved_classes.reshape(classes.shape))


def per_device(krylov, fitness_class, rate_index):
    length = krylov.shape[1]
    local_bits = length.bit_length() - 1
    wide_bits = lax.axis_size("wide").bit_length() - 1
    narrow_bits = lax.axis_size("narrow").bit_length() - 1
    remote_bits = wide_bits + narrow_bits
    common_bits = local_bits - remote_bits
    mutation = mutation_rates(rate_index, local_bits + remote_bits)
    vectors = krylov
    moved_classes = fitness_class
    at_home = True
    first_done = False
    for iteration in range(ITERS):
        if at_home:
            vectors = apply_fitness(vectors, fitness_class)
            vectors = mix_range(vectors, mutation, 0, local_bits, 0)
            vectors, moved_classes = first_move(vectors, fitness_class)
            first_done = True
            vectors = mix_range(vectors, mutation, common_bits, remote_bits, remote_bits)
        else:
            vectors = apply_fitness(vectors, moved_classes)
            vectors = mix_range(vectors, mutation, 0, common_bits, 0)
            vectors = mix_range(vectors, mutation, common_bits, remote_bits, remote_bits)
            vectors = later_move(vectors)
            vectors = mix_range(vectors, mutation, common_bits, remote_bits, 0)
        at_home = not at_home
    return vectors


def solution(mesh):
    in_specs = (P(None, ("wide", "narrow")), P(("wide", "narrow")), P())
    out_specs = P(None, ("wide", "narrow"))
    return jax.shard_map(
        per_device, mesh=mesh, in_specs=in_specs, out_specs=out_specs, check_vma=False
    )
```

profile of v0, /device:TPU:9, one launch (start us, length us, event | category | flops | bytes accessed | tf_op | source)
XLA Modules:
  0.0 456.3 jit_solution(9046856361937410167)
XLA Ops:
  1.5 6.6 %all-to-all-start.2 = ((s32[1,16,2,512]{3,2,0,1:T(2,128)}), s32[1,16,2,512]{3,2,0,1:T(2,128)S(1)}, u32[]{:S(2)}, u32[]{:S(2)}) async-start(s32[1,16,2,512]{3,2,0,1:T(2,128)} %reshape.922), calls=%async_computation.2 | async-start | bytes 131072 | tf_op jit(solution)/shard_map/all_to_all | solution.py:99
  16.9 6.1 %fusion = f32[2,4096,128]{2,1,0:T(8,128)S(1)} fusion(f32[1,2,4096,128]{3,1,2,0:T(2,128)} %bitcast.164, f32[4096,128]{1,0:T(8,128)S(1)} %copy.12, f32[2]{0:T(128)S(1)} %get-tuple-element.41, f32[2]{0:T(128)S(1)} %get-tuple-element.22, f32[2]{0:T(128)S(1)} %get-tuple-element.42, f32[2]{0:T(128)S(1)} %get-tuple-element.23, f32[2]{0:T(128)S(1)} %get-tuple-element.49, ...), kind=kOutput, calls=%fused_computation.5 | convolution fusion | flops 1612087296 | bytes 10600560 | tf_op jit(solution)/shard_map/aij,ahj->ahi/dot_general | solution.py:45
  22.9 5.3 %convolution_bitcast_fusion.5 = f32[2,64,64,128]{3,2,1,0:T(8,128)} fusion(f32[2,64,64,128]{3,2,1,0:T(8,128)S(1)} %bitcast.161, f32[2]{0:T(128)S(1)} %get-tuple-element.35, f32[2]{0:T(128)S(1)} %get-tuple-element.16, f32[2]{0:T(128)S(1)} %get-tuple-element.36, f32[2]{0:T(128)S(1)} %get-tuple-element.17, f32[2]{0:T(128)S(1)} %get-tuple-element.37, ...), kind=kOutput, calls=%fused_computation.10 | convolution fusion | flops 805396480 | bytes 8413280 | tf_op jit(solution)/shard_map/aij,ahjl->ahil/dot_general | solution.py:48
  28.2 5.4 %reshape.920 = f32[2,64,8192]{2,1,0:T(8,128)} reshape(f32[2,64,64,128]{3,2,1,0:T(8,128)} %convolution_bitcast_fusion.5) | data formatting | bytes 8388608 | tf_op jit(solution)/shard_map/reshape
  33.6 8.1 %convolution_bitcast_fusion.3 = f32[2,1,64,8192]{3,2,0,1:T(8,128)} fusion(f32[2,64,8192]{2,1,0:T(8,128)} %reshape.920, f32[2]{0:T(128)S(1)} %get-tuple-element.29, f32[2]{0:T(128)S(1)} %get-tuple-element.10, f32[2]{0:T(128)S(1)} %get-tuple-element.30, f32[2]{0:T(128)S(1)} %get-tuple-element.11, f32[2]{0:T(128)S(1)} %get-tuple-element.31, ...), kind=kOutput, calls=%fused_computation.3 | convolution fusion | flops 805396480 | bytes 8413280 | tf_op jit(solution)/shard_map/aij,ahjl->ahil/dot_general | solution.py:48
  41.8 6.0 %reshape_reshape.22 = f32[2,16,2,16384]{3,2,1,0:T(2,128)} reshape(f32[2,1,64,8192]{3,2,0,1:T(8,128)} %convolution_bitcast_fusion.3) | data formatting | bytes 8388608 | tf_op jit(solution)/shard_map/reshape;reshape | solution.py:68
  47.8 4.7 %copy.13 = f32[2,16,2,16384]{3,2,0,1:T(2,128)} copy(f32[2,16,2,16384]{3,2,1,0:T(2,128)} %reshape_reshape.22) | data formatting | bytes 8388608 | tf_op jit(solution)/shard_map/reshape;reshape | solution.py:68
  52.4 6.0 %all-to-all-start = ((f32[2,16,2,16384]{3,2,0,1:T(2,128)}), f32[2,16,2,16384]{3,2,0,1:T(2,128)}, u32[]{:S(2)}, u32[]{:S(2)}) async-start(f32[2,16,2,16384]{3,2,0,1:T(2,128)} %copy.13), calls=%async_computation | async-start | bytes 8388608 | tf_op jit(solution)/shard_map/all_to_all | solution.py:92
  59.1 89.7 %all-to-all-done = f32[2,16,2,16384]{3,2,0,1:T(2,128)} async-done(((f32[2,16,2,16384]{3,2,0,1:T(2,128)}), f32[2,16,2,16384]{3,2,0,1:T(2,128)}, u32[]{:S(2)}, u32[]{:S(2)}) %all-to-all-start) | async-done | bytes 4194336 | tf_op jit(solution)/shard_map/all_to_all | solution.py:92
  148.7 3.3 all-to-all-start.3
  152.0 6.6 %copy.14 = f32[2,16,2,16384]{3,1,0,2:T(8,128)} copy(f32[2,16,2,16384]{3,2,0,1:T(2,128)} %all-to-all-done) | data formatting | bytes 8388608 | tf_op jit(solution)/shard_map/all_to_all | solution.py:92
  158.7 5.6 %all-to-all-start.1 = ((f32[2,16,2,16384]{3,1,0,2:T(8,128)}), f32[2,16,2,16384]{3,1,0,2:T(8,128)}, u32[]{:S(2)}, u32[]{:S(2)}) async-start(f32[2,16,2,16384]{3,1,0,2:T(8,128)} %copy.14), calls=%async_computation.1 | async-start | bytes 8388608 | tf_op jit(solution)/shard_map/all_to_all | solution.py:91
  164.7 2.2 add.27
  169.8 41.1 %all-to-all-done.1 = f32[2,16,2,16384]{3,1,0,2:T(8,128)} async-done(((f32[2,16,2,16384]{3,1,0,2:T(8,128)}), f32[2,16,2,16384]{3,1,0,2:T(8,128)}, u32[]{:S(2)}, u32[]{:S(2)}) %all-to-all-start.1) | async-done | bytes 4194336 | tf_op jit(solution)/shard_map/all_to_all | solution.py:91
  210.9 7.4 %copy.15 = f32[2,16,2,16384]{3,2,1,0:T(2,128)} copy(f32[2,16,2,16384]{3,1,0,2:T(8,128)} %all-to-all-done.1) | data formatting | bytes 8388608 | tf_op jit(solution)/shard_map/all_to_all | solution.py:91
  218.3 6.1 %reshape.921 = f32[2,32,16384]{2,1,0:T(8,128)} reshape(f32[2,16,2,16384]{3,2,1,0:T(2,128)} %copy.15) | data formatting | bytes 8388608 | tf_op jit(solution)/shard_map/reshape.2
  224.4 7.9 %convolution_bitcast_fusion.2 = f32[2,1,32,16384]{3,2,0,1:T(8,128)} fusion(f32[2,32,16384]{2,1,0:T(8,128)} %reshape.921, f32[2]{0:T(128)S(1)} %get-tuple-element.25, f32[2]{0:T(128)S(1)} %get-tuple-element.6, f32[2]{0:T(128)S(1)} %get-tuple-element.26, f32[2]{0:T(128)S(1)} %get-tuple-element.7, f32[2]{0:T(128)S(1)} %get-tuple-element.27, ...), kind=kOutput, calls=%fused_computation.2 | convolution fusion | flops 402671616 | bytes 8393808 | tf_op jit(solution)/shard_map/aij,ahjl->ahil/dot_general | solution.py:48
  232.3 5.2 %reshape_reshape.23 = f32[2,4096,128]{2,1,0:T(8,128)} reshape(f32[2,1,32,16384]{3,2,0,1:T(8,128)} %convolution_bitcast_fusion.2) | data formatting | bytes 8388608 | tf_op jit(solution)/shard_map/reshape;reshape | solution.py:60
  237.5 6.6 %fusion.2 = f32[2,4096,128]{2,1,0:T(8,128)S(1)} fusion(f32[2,4096,128]{2,1,0:T(8,128)} %reshape_reshape.23, f32[4096,128]{1,0:T(8,128)S(1)} %copy-done, f32[2]{0:T(128)S(1)} %get-tuple-element.41, f32[2]{0:T(128)S(1)} %get-tuple-element.22, f32[2]{0:T(128)S(1)} %get-tuple-element.42, f32[2]{0:T(128)S(1)} %get-tuple-element.23, f32[2]{0:T(128)S(1)} %get-tuple-element.49, ...), kind=kOutput, calls=%fused_computation.7 | convolution fusion | flops 1612087296 | bytes 10600560 | tf_op jit(solution)/shard_map/aij,ahj->ahi/dot_general | solution.py:45
  244.1 8.5 %convolution_bitcast_fusion.4 = f32[2,32,128,128]{2,3,1,0:T(8,128)} fusion(f32[2,32,128,128]{3,2,1,0:T(8,128)S(1)} %bitcast.160, f32[2]{0:T(128)S(1)} %get-tuple-element.34, f32[2]{0:T(128)S(1)} %get-tuple-element.15, f32[2]{0:T(128)S(1)} %get-tuple-element.35, f32[2]{0:T(128)S(1)} %get-tuple-element.16, f32[2]{0:T(128)S(1)} %get-tuple-element.36, ...), kind=kOutput, calls=%fused_computation.9 | convolution fusion | flops 1611038720 | bytes 8503408 | tf_op jit(solution)/shard_map/aij,ahjl->ahil/dot_general | solution.py:48
  252.6 5.6 %copy.21 = f32[2,32,128,128]{3,2,1,0:T(8,128)} copy(f32[2,32,128,128]{2,3,1,0:T(8,128)} %convolution_bitcast_fusion.4) | data formatting | bytes 8388608 | tf_op jit(solution)/shard_map/aij,ahjl->ahil/transpose | solution.py:48
  258.2 5.2 %reshape.923 = f32[2,32,16384]{2,1,0:T(8,128)} reshape(f32[2,32,128,128]{3,2,1,0:T(8,128)} %copy.21) | data formatting | bytes 8388608 | tf_op jit(solution)/shard_map/reshape.8
  263.4 7.8 %convolution_bitcast_fusion.1 = f32[2,1,32,16384]{3,2,0,1:T(8,128)} fusion(f32[2,32,16384]{2,1,0:T(8,128)} %reshape.923, f32[2]{0:T(128)S(1)} %get-tuple-element.25, f32[2]{0:T(128)S(1)} %get-tuple-element.6, f32[2]{0:T(128)S(1)} %get-tuple-element.26, f32[2]{0:T(128)S(1)} %get-tuple-element.7, f32[2]{0:T(128)S(1)} %get-tuple-element.27, ...), kind=kOutput, calls=%fused_computation.1 | convolution fusion | flops 402671616 | bytes 8393808 | tf_op jit(solution)/shard_map/aij,ahjl->ahil/dot_general | solution.py:48
  271.2 5.8 %reshape_reshape.25 = f32[2,16,2,16384]{3,2,1,0:T(2,128)} reshape(f32[2,1,32,16384]{3,2,0,1:T(8,128)} %convolution_bitcast_fusion.1) | data formatting | bytes 8388608 | tf_op jit(solution)/shard_map/reshape;reshape | solution.py:68
  277.1 2.5 copy.22
  279.5 101.2 %all_to_all.30 = f32[2,16,2,16384]{3,2,0,1:T(2,128)S(1)} all-to-all(f32[2,16,2,16384]{3,2,0,1:T(2,128)S(1)} %copy.22), channel_id=1, replica_groups=mesh['wide'=16,'narrow'=2] {'wide'}, dimensions={1} | all-to-all | bytes 8388608 | tf_op jit(solution)/shard_map/all_to_all | solution.py:75
  380.8 2.4 copy.23
  383.2 50.5 %all_to_all.31 = f32[2,16,2,16384]{3,1,0,2:T(8,128)S(1)} all-to-all(f32[2,16,2,16384]{3,1,0,2:T(8,128)S(1)} %copy.23), channel_id=1, replica_groups=mesh['wide'=16,'narrow'=2] {'narrow'}, dimensions={2} | all-to-all | bytes 8388608 | tf_op jit(solution)/shard_map/all_to_all | solution.py:74
  433.7 5.2 %copy.24 = f32[2,16,2,16384]{3,2,1,0:T(2,128)} copy(f32[2,16,2,16384]{3,1,0,2:T(8,128)S(1)} %all_to_all.31) | data formatting | bytes 8388608 | tf_op jit(solution)/shard_map/all_to_all | solution.py:74
  439.0 6.1 %reshape.924 = f32[2,32,16384]{2,1,0:T(8,128)} reshape(f32[2,16,2,16384]{3,2,1,0:T(2,128)} %copy.24) | data formatting | bytes 8388608 | tf_op jit(solution)/shard_map/reshape.10
  445.0 5.5 %convolution_bitcast_fusion = f32[1,2,32,16384]{3,2,1,0:T(8,128)S(1)} fusion(f32[2,32,16384]{2,1,0:T(8,128)} %reshape.924, f32[2]{0:T(128)S(1)} %get-tuple-element.29, f32[2]{0:T(128)S(1)} %get-tuple-element.10, f32[2]{0:T(128)S(1)} %get-tuple-element.30, f32[2]{0:T(128)S(1)} %get-tuple-element.11, f32[2]{0:T(128)S(1)} %get-tuple-element.31, ...), kind=kOutput, calls=%fused_computation | convolution fusion | flops 402671616 | bytes 8393808 | tf_op jit(solution)/shard_map/aij,ahjl->ahil/dot_general | solution.py:48
  450.6 5.2 %copy.29 = f32[1,2,32,16384]{3,1,2,0:T(2,128)} copy(f32[1,2,32,16384]{3,2,1,0:T(8,128)S(1)} %convolution_bitcast_fusion) | data formatting | bytes 8388608
  (51 shorter events, 13.9 us)
Async XLA Ops:
  1.5 50.9 %all-to-all-start.2 = ((s32[1,16,2,512]{3,2,0,1:T(2,128)}), s32[1,16,2,512]{3,2,0,1:T(2,128)S(1)}, u32[]{:S(2)}, u32[]{:S(2)}) async-start(s32[1,16,2,512]{3,2,0,1:T(2,128)} %reshape.922), calls=%async_computation.2 | async-start | bytes 131072 | tf_op jit(solution)/shard_map/all_to_all | solution.py:99
  52.4 96.3 %all-to-all-start = ((f32[2,16,2,16384]{3,2,0,1:T(2,128)}), f32[2,16,2,16384]{3,2,0,1:T(2,128)}, u32[]{:S(2)}, u32[]{:S(2)}) async-start(f32[2,16,2,16384]{3,2,0,1:T(2,128)} %copy.13), calls=%async_computation | async-start | bytes 8388608 | tf_op jit(solution)/shard_map/all_to_all | solution.py:92
  148.7 9.9 %all-to-all-start.3 = ((s32[1,16,2,512]{3,1,0,2:T(8,128)}), s32[1,16,2,512]{3,1,0,2:T(8,128)S(1)}, u32[]{:S(2)}, u32[]{:S(2)}) async-start(s32[1,16,2,512]{3,1,0,2:T(8,128)} %copy.16), calls=%async_computation.3 | async-start | bytes 131072 | tf_op jit(solution)/shard_map/all_to_all | solution.py:98
  158.7 52.2 %all-to-all-start.1 = ((f32[2,16,2,16384]{3,1,0,2:T(8,128)}), f32[2,16,2,16384]{3,1,0,2:T(8,128)}, u32[]{:S(2)}, u32[]{:S(2)}) async-start(f32[2,16,2,16384]{3,1,0,2:T(8,128)} %copy.14), calls=%async_computation.1 | async-start | bytes 8388608 | tf_op jit(solution)/shard_map/all_to_all | solution.py:91
  232.3 5.2 %copy-start = (f32[4096,128]{1,0:T(8,128)S(1)}, f32[4096,128]{1,0:T(8,128)}, u32[]{:S(2)}) copy-start(f32[4096,128]{1,0:T(8,128)} %copy.19) | copy-start | bytes 6291460
where the time goes:
time: 465 us; the launch traced here: 456 us
  blocking collectives  152 us (33%)
  waiting for transfers between devices  131 us (28%)
  local copies, waits for them, and re-layouts  93 us (20%)
  matrix products  55.8 us (12%)
  starting transfers between devices  21.5 us (5%)
    all_to_all x1, blocking collectives, later_move(): lax.all_to_all(device_shape(vectors), 'wide', split_axis=1, concat_axis=1...  101 us
    all_to_all x1, waiting for transfers between devices, first_move(): lax.all_to_all(device_shape(vectors), 'wide', split_axis=1, concat_axis=1...  89.7 us
    all_to_all x1, blocking collectives, later_move(): lax.all_to_all(lax.all_to_all(device_shape(vectors), 'wide', split_axis=1...  50.5 us
    dot_general x6, matrix products, mix_range(): jnp.einsum('aij,ahjl->ahil', matrix, shaped, precision=lax.Precision.HIGH...  43.2 us
    all_to_all x1, waiting for transfers between devices, first_move(): lax.all_to_all(lax.all_to_all(device_shape(vectors), 'wide', split_axis=1...  41.1 us
    another operation x4, local copies, waits for them, and re-layouts, device_shape(): vectors.reshape(vector_count, wide_count, narrow_count, length // (wide_c...  18.9 us
    another operation x3, local copies, waits for them, and re-layouts  17.3 us
    dot_general x2, matrix products, mix_range(): jnp.einsum('aij,ahj->ahi', matrix, shaped, precision=lax.Precision.HIGHEST)  12.6 us
  transfers between devices with their start and end apart: 4, of which 2 were waited for; matrix products, arithmetic and copies ran while one was open for 12% of the time, Pallas kernels for 0%

commit v1 on v0

v1 whole, which is shorter than its diff:
```python
import functools

import jax
import jax.numpy as jnp
import numpy as np
from jax import lax
from jax.experimental import pallas as pl
from jax.experimental.pallas import tpu as pltpu
from jax.sharding import PartitionSpec as P

LANES = 128
ROWS = 8
LANE_BITS = 7


def bits_of(count):
    return count.bit_length() - 1


def profile_of(total_bits):
    position = np.arange(total_bits, dtype=np.float32)
    return np.float32(1.0) + np.float32(0.5) * np.cos(np.float32(2.0) * position)


def rates_of(rate_ref, vector, profile, first, amount):
    level = 0.004 * (rate_ref[vector].astype(jnp.float32) + 1.0)
    return [level * float(profile[first + bit]) for bit in range(amount)]


def kron(rates, size):
    row = lax.broadcasted_iota(jnp.int32, (size, size), 0)
    column = lax.broadcasted_iota(jnp.int32, (size, size), 1)
    product = jnp.ones((size, size), jnp.float32)
    for bit, rate in enumerate(rates):
        agreeing = ((row >> bit) & 1) == ((column >> bit) & 1)
        product = product * jnp.where(agreeing, 1.0 - rate, rate)
    return product


def halves(values):
    high = values.astype(jnp.bfloat16)
    return high, (values - high.astype(jnp.float32)).astype(jnp.bfloat16)


def dot(left, right):
    return jnp.dot(left, right, preferred_element_type=jnp.float32)


def butterfly(values, rates):
    values = list(values)
    for bit, rate in enumerate(rates):
        step = 1 << bit
        for low in range(len(values)):
            if low & step:
                continue
            change = (values[low | step] - values[low]) * rate
            values[low] = values[low] + change
            values[low | step] = values[low | step] - change
    return values


def groups_of(bits):
    count = max(1, -(-bits // 5))
    groups, first = [], 0
    for number in range(count):
        amount = bits // count + (1 if number < bits % count else 0)
        groups.append((first, amount))
        first += amount
    return groups


def group_pass(group, bits, tiles, rates, load, store, scale=None):
    first, amount = group
    low = 1 << first
    others = (1 << bits) // (1 << amount)
    part = rates[first : first + amount]

    def body(step, carry):
        tile = step % tiles
        other = step // tiles
        base = (other // low) * (low << amount) + other % low
        index = [base + member * low for member in range(1 << amount)]
        values = butterfly([load(at, tile) for at in index], part)
        if scale is not None:
            values = [value * scale(at, tile) for value, at in zip(values, index)]
            values = butterfly(values, part)
        for at, value in zip(index, values):
            store(at, tile, value)
        return carry

    lax.fori_loop(0, others * tiles, body, 0)


def xor(left, right, bits):
    both = 0
    for bit in range(bits):
        both = both + (1 << bit) * (((left // (1 << bit)) % 2) * ((right // (1 << bit)) % 2))
    return left + right - 2 * both


def exchange_kernel(
    sizes, x_ref, class_ref, rate_ref, out_ref,
    send_a, send_b, land_a, land_b, scale_here, scale_moved, back, lane_high, lane_low,
    mid_high, mid_low, send_sem, land_sem, own_sem,
):
    wide, narrow, rows, local_bits, per_row = sizes
    count = wide * narrow
    wide_bits, narrow_bits = bits_of(wide), bits_of(narrow)
    device_bits = wide_bits + narrow_bits
    low_bits = local_bits - device_bits
    tiles = rows // ROWS
    class_rows = class_ref.shape[1]
    profile = profile_of(local_bits + device_bits)
    my_wide, my_narrow = lax.axis_index("wide"), lax.axis_index("narrow")
    me = my_wide * narrow + my_narrow

    def partner(turn):
        offset = (turn % 2) * (count // 2) + turn // 2
        to_wide = xor(my_wide, offset // narrow, wide_bits)
        to_narrow = xor(my_narrow, offset % narrow, narrow_bits)
        return offset, to_wide, to_narrow, to_wide * narrow + to_narrow

    barrier = pltpu.get_barrier_semaphore()

    def greet(turn, carry):
        _, to_wide, to_narrow, _ = partner(turn)
        pl.semaphore_signal(
            barrier, inc=1, device_id=(to_wide, to_narrow), device_id_type=pl.DeviceIdType.MESH
        )
        return carry

    lax.fori_loop(1, count, greet, 0)

    def copy(stage, turn):
        offset, to_wide, to_narrow, flat = partner(turn)
        source, target = (
            (send_a, land_a), (send_b, land_b), (back.at[0], out_ref.at[0]), (back.at[1], out_ref.at[1])
        )[stage]
        return flat, pltpu.make_async_remote_copy(
            src_ref=source.at[flat],
            dst_ref=target.at[me],
            send_sem=send_sem.at[stage, offset],
            recv_sem=land_sem.at[stage, offset],
            device_id=(to_wide, to_narrow),
            device_id_type=pl.DeviceIdType.MESH,
        )

    for vector in range(2):
        for high_ref, low_ref, first, size in (
            (lane_high, lane_low, 0, LANES),
            (mid_high, mid_low, LANE_BITS, rows),
        ):
            rates = rates_of(rate_ref, vector, profile, first, bits_of(size))
            high_ref[vector], low_ref[vector] = halves(kron(rates, size))

    def expand(compact):
        span = min(rows, LANES // per_row)
        spread = jnp.concatenate(
            [jnp.broadcast_to(compact[at : at + 1], (span, LANES)) for at in range(class_rows)], axis=0
        )
        row = lax.broadcasted_iota(jnp.int32, (rows, LANES), 0)
        column = lax.broadcasted_iota(jnp.int32, (rows, LANES), 1)
        kept = jnp.where(row % span == column // per_row, spread, 0.0).astype(jnp.bfloat16)
        source = lax.broadcasted_iota(jnp.int32, (LANES, LANES), 0)
        lane = lax.broadcasted_iota(jnp.int32, (LANES, LANES), 1)
        pick = jnp.where(source % per_row == lane // (LANES // per_row), 1.0, 0.0)
        return dot(kept, pick.astype(jnp.bfloat16))

    def spread_here(at, carry):
        compact = 0.5 + 0.25 * class_ref[at].astype(jnp.float32)
        send_a[at, rows:, :] = jnp.concatenate(
            [compact, jnp.zeros((ROWS - class_rows, LANES), jnp.float32)], axis=0
        )
        scale_here[at] = expand(compact)
        return carry

    lax.fori_loop(0, count, spread_here, 0)

    def tile_rows(tile):
        return pl.ds(pl.multiple_of(tile * ROWS, ROWS), ROWS)

    def prepare(vector, target):
        rates = rates_of(rate_ref, vector, profile, low_bits, device_bits)
        groups = groups_of(device_bits)

        def first_load(at, tile):
            start = 2 * (at * rows + tile * ROWS) + vector
            return x_ref[pl.ds(start, ROWS, stride=2), :] * scale_here[at, tile_rows(tile), :]

        def load(at, tile):
            return target[at, tile_rows(tile), :]

        def store(at, tile, value):
            target[at, tile_rows(tile), :] = value

        for number, group in enumerate(groups):
            group_pass(group, device_bits, tiles, rates, load if number else first_load, store)

    def low_mix(values, vector):
        high, low = halves(values)
        right = lane_high[vector]
        values = dot(high, right) + (dot(low, right) + dot(high, lane_low[vector]))
        high, low = halves(values)
        left = mid_high[vector]
        return dot(left, high) + (dot(left, low) + dot(mid_low[vector], high))

    def turn_over(vector, held):
        rates = rates_of(rate_ref, vector, profile, local_bits, device_bits)
        groups = groups_of(device_bits)

        def load(at, tile):
            return held[at, tile_rows(tile), :]

        def store(at, tile, value):
            held[at, tile_rows(tile), :] = value

        def scale(at, tile):
            return scale_moved[at, tile_rows(tile), :]

        for group in groups[:-1]:
            group_pass(group, device_bits, tiles, rates, load, store)
        group_pass(groups[-1], device_bits, tiles, rates, load, store, scale)
        for group in groups[:-1]:
            group_pass(group, device_bits, tiles, rates, load, store)

    prepare(0, send_a)
    pl.semaphore_wait(barrier, count - 1)

    def start_first(turn, carry):
        copy(0, turn)[1].start()
        return carry

    lax.fori_loop(1, count, start_first, 0)
    prepare(1, send_b)

    land_a[me, :rows, :] = low_mix(send_a[me, :rows, :], 0)
    scale_moved[me] = expand(send_a[me, rows : rows + class_rows, :])

    def first_arrivals(turn, carry):
        flat, arriving = copy(0, turn)
        arriving.wait_send()
        copy(1, turn)[1].start()
        arriving.wait_recv()
        land_a[flat, :rows, :] = low_mix(land_a[flat, :rows, :], 0)
        scale_moved[flat] = expand(land_a[flat, rows : rows + class_rows, :])
        return carry

    lax.fori_loop(1, count, first_arrivals, 0)
    turn_over(0, land_a)

    land_b[me] = low_mix(send_b[me], 1)
    back[0, me] = low_mix(land_a[me, :rows, :], 0)
    own_first = pltpu.make_async_copy(back.at[0, me], out_ref.at[0, me], own_sem.at[0])
    own_first.start()

    def second_arrivals(turn, carry):
        flat, arriving = copy(1, turn)
        back[0, flat] = low_mix(land_a[flat, :rows, :], 0)
        arriving.wait_send()
        copy(2, turn)[1].start()
        arriving.wait_recv()
        land_b[flat] = low_mix(land_b[flat], 1)
        return carry

    lax.fori_loop(1, count, second_arrivals, 0)
    turn_over(1, land_b)

    back[1, me] = low_mix(land_b[me], 1)
    own_second = pltpu.make_async_copy(back.at[1, me], out_ref.at[1, me], own_sem.at[1])
    own_second.start()

    def third_arrivals(turn, carry):
        flat, arriving = copy(2, turn)
        back[1, flat] = low_mix(land_b[flat], 1)
        arriving.wait_send()
        copy(3, turn)[1].start()
        return carry

    lax.fori_loop(1, count, third_arrivals, 0)
    own_first.wait()
    own_second.wait()

    def last_arrivals(turn, carry):
        copy(2, turn)[1].wait_recv()
        copy(3, turn)[1].wait()
        return carry

    lax.fori_loop(1, count, last_arrivals, 0)


def finish_kernel(sizes, profile, land_ref, rate_ref, out_ref, held):
    device_bits, low_bits = sizes
    tiles = land_ref.shape[2] // ROWS
    groups = groups_of(device_bits)

    def tile_rows(tile):
        return pl.ds(pl.multiple_of(tile * ROWS, ROWS), ROWS)

    for vector in range(2):
        rates = rates_of(rate_ref, vector, profile, low_bits, device_bits)

        def first_load(at, tile):
            return land_ref[vector, at, tile_rows(tile), :]

        def load(at, tile):
            return held[at, tile_rows(tile), :]

        def store(at, tile, value):
            held[at, tile_rows(tile), :] = value

        def last_store(at, tile, value):
            out_ref[at, pl.ds(2 * ROWS * tile + vector, ROWS, stride=2), :] = value

        for number, group in enumerate(groups):
            group_pass(
                group, device_bits, tiles, rates,
                load if number else first_load,
                last_store if number == len(groups) - 1 else store,
            )


def per_device(krylov, fitness_class, rate_index):
    vectors, length = krylov.shape
    wide, narrow = lax.axis_size("wide"), lax.axis_size("narrow")
    count = wide * narrow
    local_bits, device_bits = bits_of(length), bits_of(count)
    low_bits = local_bits - device_bits
    slab = length // count
    rows = slab // LANES
    per_row = LANES * fitness_class.shape[0] // length
    slab_classes = fitness_class.shape[0] // count
    interleaved = krylov.reshape(vectors, length // LANES, LANES).transpose(1, 0, 2)
    interleaved = interleaved.reshape(vectors * length // LANES, LANES)
    classes = fitness_class.reshape(count, slab_classes)
    if slab_classes < LANES:
        classes = jnp.pad(classes, ((0, 0), (0, LANES - slab_classes)))
    classes = classes.reshape(count, -1, LANES)
    f32, bf16 = jnp.float32, jnp.bfloat16
    vmem = pl.BlockSpec(memory_space=pltpu.VMEM)
    smem = pl.BlockSpec(memory_space=pltpu.SMEM)
    landed = pl.pallas_call(
        functools.partial(exchange_kernel, (wide, narrow, rows, local_bits, per_row)),
        out_shape=jax.ShapeDtypeStruct((vectors, count, rows, LANES), f32),
        in_specs=[vmem, vmem, smem],
        out_specs=pl.BlockSpec(memory_space=pl.ANY),
        scratch_shapes=[
            pltpu.VMEM((count, rows + ROWS, LANES), f32),
            pltpu.VMEM((count, rows, LANES), f32),
            pltpu.VMEM((count, rows + ROWS, LANES), f32),
            pltpu.VMEM((count, rows, LANES), f32),
            pltpu.VMEM((count, rows, LANES), f32),
            pltpu.VMEM((count, rows, LANES), f32),
            pltpu.VMEM((vectors, count, rows, LANES), f32),
            pltpu.VMEM((vectors, LANES, LANES), bf16),
            pltpu.VMEM((vectors, LANES, LANES), bf16),
            pltpu.VMEM((vectors, rows, rows), bf16),
            pltpu.VMEM((vectors, rows, rows), bf16),
            pltpu.SemaphoreType.DMA((4, count)),
            pltpu.SemaphoreType.DMA((4, count)),
            pltpu.SemaphoreType.DMA((2,)),
        ],
        compiler_params=pltpu.CompilerParams(
            collective_id=0, has_side_effects=True, vmem_limit_bytes=44 * 1024 * 1024
        ),
        name="exchange",
    )(interleaved, classes, rate_index)

    block = min(rows, 32)
    profile = profile_of(local_bits + device_bits)
    mixed = pl.pallas_call(
        functools.partial(finish_kernel, (device_bits, low_bits), profile),
        grid=(rows // block,),
        out_shape=jax.ShapeDtypeStruct((count, vectors * rows, LANES), f32),
        in_specs=[
            pl.BlockSpec((vectors, count, block, LANES), lambda step: (0, 0, step, 0)),
            smem,
        ],
        out_specs=pl.BlockSpec((count, vectors * block, LANES), lambda step: (0, step, 0)),
        scratch_shapes=[pltpu.VMEM((count, block, LANES), f32)],
        compiler_params=pltpu.CompilerParams(vmem_limit_bytes=40 * 1024 * 1024),
        name="finish",
    )(landed, rate_index)
    mixed = mixed.reshape(length // LANES, vectors, LANES).transpose(1, 0, 2)
    return mixed.reshape(vectors, length)


def solution(mesh):
    in_specs = (P(None, ("wide", "narrow")), P(("wide", "narrow")), P())
    out_specs = P(None, ("wide", "narrow"))
    return jax.shard_map(
        per_device, mesh=mesh, in_specs=in_specs, out_specs=out_specs, check_vma=False
    )
```

time: 465 us -> 206 us (0.44); the launches traced: 456 us -> 206 us
  Pallas kernels: 0 us -> 202 us
  blocking collectives: 152 us -> 0 us
  waiting for transfers between devices: 131 us -> 0 us
  local copies, waits for them, and re-layouts: 93 us -> 3.68 us
  matrix products: 55.8 us -> 0 us
  starting transfers between devices: 21.5 us -> 0 us
    pallas_call x0 -> x2, Pallas kernels: none -> 202 us  [the longest x1 198 us: per_device(): pl.pallas_call(functools.partial(exchange_kernel, (wide, narrow, rows, lo...]
    all_to_all x2 -> x0, blocking collectives: 152 us -> none  [the longest x1 101 us: later_move(): lax.all_to_all(device_shape(vectors), 'wide', split_axis=1, concat_axis=1...]
    all_to_all x4 -> x0, waiting for transfers between devices: 131 us -> none  [the longest x1 89.7 us: first_move(): lax.all_to_all(device_shape(vectors), 'wide', split_axis=1, concat_axis=1...]
    dot_general x8 -> x0, matrix products: 55.8 us -> none  [the longest x6 43.2 us: mix_range(): jnp.einsum('aij,ahjl->ahil', matrix, shaped, precision=lax.Precision.HIGH...]
    another operation x10 -> x0, local copies, waits for them, and re-layouts: 41.4 us -> none  [the longest x4 18.9 us: device_shape(): vectors.reshape(vector_count, wide_count, narrow_count, length // (wide_c...]
    all_to_all x5 -> x0, local copies, waits for them, and re-layouts: 22.4 us -> none  [the longest x1 7.44 us: first_move(): lax.all_to_all(lax.all_to_all(device_shape(vectors), 'wide', split_axis=1...]
    all_to_all x4 -> x0, starting transfers between devices: 21.5 us -> none  [the longest x1 6.58 us: first_move(): lax.all_to_all(class_shaped, 'wide', split_axis=1, concat_axis=1, tiled=T...]
    mul x6 -> x0, local copies, waits for them, and re-layouts: 8.45 us -> none  [apply_fitness(): vectors.reshape(vector_count, blocks, length // blocks)]
  transfers between devices with their start and end apart: 4 -> 0, of which waited for: 2 -> 0; matrix products, arithmetic and copies ran while one was open for 12% -> 0% of each run, Pallas kernels for 0% -> 0%
where the time goes in v1:
time: 206 us
  Pallas kernels  202 us (98%)
  local copies, waits for them, and re-layouts  3.68 us (2%)
    pallas_call x1, Pallas kernels, per_device(): pl.pallas_call(functools.partial(exchange_kernel, (wide, narrow, rows, lo...  198 us
    pallas_call x1, Pallas kernels, per_device(): pl.pallas_call(functools.partial(finish_kernel, (device_bits, low_bits),...  4.26 us

profile of v1, /device:TPU:9, one launch (start us, length us, event | category | flops | bytes accessed | tf_op | source)
XLA Modules:
  0.0 205.9 jit_solution(773063729280906308)
XLA Ops:
  0.0 0.0 copy-start
  0.0 2.2 %copy-done = f32[2,524288]{1,0:T(2,128)S(1)} copy-done((f32[2,524288]{1,0:T(2,128)S(1)}, f32[2,524288]{1,0:T(2,128)}, u32[]{:S(2)}) %copy-start) | copy-done | bytes 4194328
  2.2 0.0 copy-start.1
  2.2 0.8 copy-done.1
  3.0 0.0 copy-start.2
  3.0 0.7 copy-done.2
  3.7 197.9 %exchange.1.land_ref = f32[2,32,128,128]{3,2,1,0:T(8,128)S(1)} custom-call(f32[8192,128]{1,0:T(8,128)S(1)} %bitcast.11, s32[32,4,128]{2,1,0:T(4,128)S(1)} %bitcast.12, s32[2]{0:T(128)S(1)} %copy-done.2), custom_call_target="tpu_custom_call" | custom-call | tf_op jit(solution)/shard_map/exchange/pallas_call | solution.py:341
  201.6 4.3 %finish.1 = f32[32,256,128]{2,1,0:T(8,128)} custom-call(f32[2,32,128,128]{3,2,1,0:T(8,128)S(1)} %exchange.1.land_ref, s32[2]{0:T(128)S(1)} %copy-done.2), custom_call_target="tpu_custom_call" | custom-call | tf_op jit(solution)/shard_map/finish/pallas_call | solution.py:370
Async XLA Ops:
  0.0 2.2 %copy-start = (f32[2,524288]{1,0:T(2,128)S(1)}, f32[2,524288]{1,0:T(2,128)}, u32[]{:S(2)}) copy-start(f32[2,524288]{1,0:T(2,128)} %param.3) | copy-start | bytes 12582916
  2.2 0.8 copy-start.1
  3.0 0.7 copy-start.2

commit v2 on v1

--- a/solution.py
+++ b/solution.py
@@ -114,7 +114,10 @@
     my_wide, my_narrow = lax.axis_index("wide"), lax.axis_index("narrow")
     me = my_wide * narrow + my_narrow
 
+    swapped = my_wide % 2
+
     def partner(turn):
+        turn = turn + swapped * (2 * (turn % 2) - 1) * (1 - turn // (count - 1))
         offset = (turn % 2) * (count // 2) + turn // 2
         to_wide = xor(my_wide, offset // narrow, wide_bits)
         to_narrow = xor(my_narrow, offset % narrow, narrow_bits)

time: 206 us -> 207 us (level)
  no operation moved by 1% of the time
where the time goes in v2:
time: 207 us; the launch traced here: 206 us
  Pallas kernels  203 us (98%)
  local copies, waits for them, and re-layouts  3.68 us (2%)
    pallas_call x1, Pallas kernels, per_device(): pl.pallas_call(functools.partial(exchange_kernel, (wide, narrow, rows, lo...  198 us
    pallas_call x1, Pallas kernels, per_device(): pl.pallas_call(functools.partial(finish_kernel, (device_bits, low_bits),...  4.26 us

profile of v2, /device:TPU:9, one launch (start us, length us, event | category | flops | bytes accessed | tf_op | source)
XLA Modules:
  0.0 206.3 jit_solution(18228865175811681295)
XLA Ops:
  0.0 0.0 copy-start
  0.0 2.2 %copy-done = f32[2,524288]{1,0:T(2,128)S(1)} copy-done((f32[2,524288]{1,0:T(2,128)S(1)}, f32[2,524288]{1,0:T(2,128)}, u32[]{:S(2)}) %copy-start) | copy-done | bytes 4194328
  2.2 0.0 copy-start.1
  2.2 0.8 copy-done.1
  3.0 0.0 copy-start.2
  3.0 0.7 copy-done.2
  3.7 198.4 %exchange.1.land_ref = f32[2,32,128,128]{3,2,1,0:T(8,128)S(1)} custom-call(f32[8192,128]{1,0:T(8,128)S(1)} %bitcast.11, s32[32,4,128]{2,1,0:T(4,128)S(1)} %bitcast.12, s32[2]{0:T(128)S(1)} %copy-done.2), custom_call_target="tpu_custom_call" | custom-call | tf_op jit(solution)/shard_map/exchange/pallas_call | solution.py:344
  202.1 4.3 %finish.1 = f32[32,256,128]{2,1,0:T(8,128)} custom-call(f32[2,32,128,128]{3,2,1,0:T(8,128)S(1)} %exchange.1.land_ref, s32[2]{0:T(128)S(1)} %copy-done.2), custom_call_target="tpu_custom_call" | custom-call | tf_op jit(solution)/shard_map/finish/pallas_call | solution.py:373
Async XLA Ops:
  0.0 2.2 %copy-start = (f32[2,524288]{1,0:T(2,128)S(1)}, f32[2,524288]{1,0:T(2,128)}, u32[]{:S(2)}) copy-start(f32[2,524288]{1,0:T(2,128)} %param.3) | copy-start | bytes 12582916
  2.2 0.8 copy-start.1
  3.0 0.7 copy-start.2

commit v3 on v1

--- a/solution.py
+++ b/solution.py
@@ -69,14 +69,14 @@
     return groups
 
 
-def group_pass(group, bits, tiles, rates, load, store, scale=None):
+def group_pass(group, bits, tiles, rates, load, store, scale=None, first_tile=0):
     first, amount = group
     low = 1 << first
     others = (1 << bits) // (1 << amount)
     part = rates[first : first + amount]
 
     def body(step, carry):
-        tile = step % tiles
+        tile = first_tile + step % tiles
         other = step // tiles
         base = (other // low) * (low << amount) + other % low
         index = [base + member * low for member in range(1 << amount)]
@@ -99,9 +99,9 @@
 
 
 def exchange_kernel(
-    sizes, x_ref, class_ref, rate_ref, out_ref,
+    sizes, x_hbm, class_ref, rate_ref, out_ref,
     send_a, send_b, land_a, land_b, scale_here, scale_moved, back, lane_high, lane_low,
-    mid_high, mid_low, send_sem, land_sem, own_sem,
+    mid_high, mid_low, held, send_sem, land_sem, own_sem, load_sem,
 ):
     wide, narrow, rows, local_bits, per_row = sizes
     count = wide * narrow
@@ -119,6 +119,16 @@
         to_wide = xor(my_wide, offset // narrow, wide_bits)
         to_narrow = xor(my_narrow, offset % narrow, narrow_bits)
         return offset, to_wide, to_narrow, to_wide * narrow + to_narrow
+
+    chunks = min(4, tiles)
+    chunk_rows = 2 * rows // chunks
+    loads = []
+    for chunk in range(chunks):
+        part = pl.ds(chunk * chunk_rows, chunk_rows)
+        loads.append(
+            pltpu.make_async_copy(x_hbm.at[:, part, :], held.at[:, part, :], load_sem.at[chunk])
+        )
+        loads[-1].start()
 
     barrier = pltpu.get_barrier_semaphore()
 
@@ -145,47 +155,61 @@
             device_id_type=pl.DeviceIdType.MESH,
         )
 
-    for vector in range(2):
-        for high_ref, low_ref, first, size in (
-            (lane_high, lane_low, 0, LANES),
-            (mid_high, mid_low, LANE_BITS, rows),
-        ):
-            rates = rates_of(rate_ref, vector, profile, first, bits_of(size))
-            high_ref[vector], low_ref[vector] = halves(kron(rates, size))
-
-    def expand(compact):
+    def build_matrices():
+        for vector in range(2):
+            for high_ref, low_ref, first, size in (
+                (lane_high, lane_low, 0, LANES),
+                (mid_high, mid_low, LANE_BITS, rows),
+            ):
+                rates = rates_of(rate_ref, vector, profile, first, bits_of(size))
+                high_ref[vector], low_ref[vector] = halves(kron(rates, size))
+
+    def expand(compacts):
         span = min(rows, LANES // per_row)
         spread = jnp.concatenate(
-            [jnp.broadcast_to(compact[at : at + 1], (span, LANES)) for at in range(class_rows)], axis=0
+            [
+                jnp.broadcast_to(compact[at : at + 1], (span, LANES))
+                for compact in compacts
+                for at in range(class_rows)
+            ],
+            axis=0,
         )
-        row = lax.broadcasted_iota(jnp.int32, (rows, LANES), 0)
-        column = lax.broadcasted_iota(jnp.int32, (rows, LANES), 1)
+        row = lax.broadcasted_iota(jnp.int32, spread.shape, 0)
+        column = lax.broadcasted_iota(jnp.int32, spread.shape, 1)
         kept = jnp.where(row % span == column // per_row, spread, 0.0).astype(jnp.bfloat16)
         source = lax.broadcasted_iota(jnp.int32, (LANES, LANES), 0)
         lane = lax.broadcasted_iota(jnp.int32, (LANES, LANES), 1)
         pick = jnp.where(source % per_row == lane // (LANES // per_row), 1.0, 0.0)
         return dot(kept, pick.astype(jnp.bfloat16))
 
-    def spread_here(at, carry):
-        compact = 0.5 + 0.25 * class_ref[at].astype(jnp.float32)
-        send_a[at, rows:, :] = jnp.concatenate(
-            [compact, jnp.zeros((ROWS - class_rows, LANES), jnp.float32)], axis=0
-        )
-        scale_here[at] = expand(compact)
+    together = min(8, count)
+
+    def spread_here(step, carry):
+        compacts = []
+        for member in range(together):
+            at = step * together + member
+            compact = 0.5 + 0.25 * class_ref[at].astype(jnp.float32)
+            send_a[at, rows:, :] = jnp.concatenate(
+                [compact, jnp.zeros((ROWS - class_rows, LANES), jnp.float32)], axis=0
+            )
+            compacts.append(compact)
+        spread = expand(compacts)
+        for member in range(together):
+            scale_here[step * together + member] = spread[member * rows : (member + 1) * rows]
         return carry
 
-    lax.fori_loop(0, count, spread_here, 0)
+    lax.fori_loop(0, count // together, spread_here, 0)
 
     def tile_rows(tile):
         return pl.ds(pl.multiple_of(tile * ROWS, ROWS), ROWS)
 
-    def prepare(vector, target):
+    def prepare(vector, target, chunk):
         rates = rates_of(rate_ref, vector, profile, low_bits, device_bits)
         groups = groups_of(device_bits)
 
         def first_load(at, tile):
-            start = 2 * (at * rows + tile * ROWS) + vector
-            return x_ref[pl.ds(start, ROWS, stride=2), :] * scale_here[at, tile_rows(tile), :]
+            pairs = pl.ds(2 * ROWS * tile + vector, ROWS, stride=2)
+            return held[at, pairs, :] * scale_here[at, tile_rows(tile), :]
 
         def load(at, tile):
             return target[at, tile_rows(tile), :]
@@ -194,15 +218,22 @@
             target[at, tile_rows(tile), :] = value
 
         for number, group in enumerate(groups):
-            group_pass(group, device_bits, tiles, rates, load if number else first_load, store)
-
-    def low_mix(values, vector):
-        high, low = halves(values)
+            group_pass(
+                group, device_bits, tiles // chunks, rates,
+                load if number else first_load, store, first_tile=chunk * (tiles // chunks),
+            )
+
+    def low_mix(slabs, vector):
+        high, low = halves(jnp.concatenate(slabs, axis=0))
         right = lane_high[vector]
         values = dot(high, right) + (dot(low, right) + dot(high, lane_low[vector]))
+        values = jnp.concatenate(
+            [values[at * rows : (at + 1) * rows] for at in range(len(slabs))], axis=1
+        )
         high, low = halves(values)
         left = mid_high[vector]
-        return dot(left, high) + (dot(left, low) + dot(mid_low[vector], high))
+        values = dot(left, high) + (dot(left, low) + dot(mid_low[vector], high))
+        return [values[:, at * LANES : (at + 1) * LANES] for at in range(len(slabs))]
 
     def turn_over(vector, held):
         rates = rates_of(rate_ref, vector, profile, local_bits, device_bits)
@@ -223,7 +254,24 @@
         for group in groups[:-1]:
             group_pass(group, device_bits, tiles, rates, load, store)
 
-    prepare(0, send_a)
+    def each_pair(step):
+        step(0, True)
+
+        def body(pair, carry):
+            step(pair, False)
+            return carry
+
+        lax.fori_loop(1, count // 2, body, 0)
+
+    def turns_of(pair, with_own):
+        return [2 * pair + 1] if with_own else [2 * pair, 2 * pair + 1]
+
+    def slabs_of(pair):
+        return [partner(2 * pair)[3], partner(2 * pair + 1)[3]]
+
+    for chunk in range(chunks):
+        loads[chunk].wait()
+        prepare(0, send_a, chunk)
     pl.semaphore_wait(barrier, count - 1)
 
     def start_first(turn, carry):
@@ -231,54 +279,63 @@
         return carry
 
     lax.fori_loop(1, count, start_first, 0)
-    prepare(1, send_b)
-
-    land_a[me, :rows, :] = low_mix(send_a[me, :rows, :], 0)
-    scale_moved[me] = expand(send_a[me, rows : rows + class_rows, :])
-
-    def first_arrivals(turn, carry):
-        flat, arriving = copy(0, turn)
-        arriving.wait_send()
-        copy(1, turn)[1].start()
-        arriving.wait_recv()
-        land_a[flat, :rows, :] = low_mix(land_a[flat, :rows, :], 0)
-        scale_moved[flat] = expand(land_a[flat, rows : rows + class_rows, :])
-        return carry
-
-    lax.fori_loop(1, count, first_arrivals, 0)
+    build_matrices()
+    for chunk in range(chunks):
+        prepare(1, send_b, chunk)
+
+    def first_arrivals(pair, with_own):
+        turns = turns_of(pair, with_own)
+        for turn in turns:
+            copy(0, turn)[1].wait_send()
+            copy(1, turn)[1].start()
+        for turn in turns:
+            copy(0, turn)[1].wait_recv()
+        slabs = slabs_of(pair)
+        sources = [send_a if with_own and not at else land_a for at in range(2)]
+        mixed = low_mix([source[flat, :rows, :] for source, flat in zip(sources, slabs)], 0)
+        spread = expand([source[flat, rows : rows + class_rows, :] for source, flat in zip(sources, slabs)])
+        for at, flat in enumerate(slabs):
+            land_a[flat, :rows, :] = mixed[at]
+            scale_moved[flat] = spread[at * rows : (at + 1) * rows]
+
+    each_pair(first_arrivals)
     turn_over(0, land_a)
 
-    land_b[me] = low_mix(send_b[me], 1)
-    back[0, me] = low_mix(land_a[me, :rows, :], 0)
-    own_first = pltpu.make_async_copy(back.at[0, me], out_ref.at[0, me], own_sem.at[0])
-    own_first.start()
-
-    def second_arrivals(turn, carry):
-        flat, arriving = copy(1, turn)
-        back[0, flat] = low_mix(land_a[flat, :rows, :], 0)
-        arriving.wait_send()
-        copy(2, turn)[1].start()
-        arriving.wait_recv()
-        land_b[flat] = low_mix(land_b[flat], 1)
-        return carry
-
-    lax.fori_loop(1, count, second_arrivals, 0)
+    own = [
+        pltpu.make_async_copy(back.at[vector, me], out_ref.at[vector, me], own_sem.at[vector])
+        for vector in range(2)
+    ]
+
+    def send_back(vector, landed, pair, with_own):
+        slabs = slabs_of(pair)
+        mixed = low_mix([landed[flat, :rows, :] for flat in slabs], vector)
+        for flat, values in zip(slabs, mixed):
+            back[vector, flat] = values
+        if with_own:
+            own[vector].start()
+        for turn in turns_of(pair, with_own):
+            copy(1 + vector, turn)[1].wait_send()
+            copy(2 + vector, turn)[1].start()
+
+    def second_arrivals(pair, with_own):
+        send_back(0, land_a, pair, with_own)
+        for turn in turns_of(pair, with_own):
+            copy(1, turn)[1].wait_recv()
+        slabs = slabs_of(pair)
+        sources = [send_b if with_own and not at else land_b for at in range(2)]
+        mixed = low_mix([source[flat] for source, flat in zip(sources, slabs)], 1)
+        for flat, values in zip(slabs, mixed):
+            land_b[flat] = values
+
+    each_pair(second_arrivals)
     turn_over(1, land_b)
 
-    back[1, me] = low_mix(land_b[me], 1)
-    own_second = pltpu.make_async_copy(back.at[1, me], out_ref.at[1, me], own_sem.at[1])
-    own_second.start()
-
-    def third_arrivals(turn, carry):
-        flat, arriving = copy(2, turn)
-        back[1, flat] = low_mix(land_b[flat], 1)
-        arriving.wait_send()
-        copy(3, turn)[1].start()
-        return carry
-
-    lax.fori_loop(1, count, third_arrivals, 0)
-    own_first.wait()
-    own_second.wait()
+    def third_arrivals(pair, with_own):
+        send_back(1, land_b, pair, with_own)
+
+    each_pair(third_arrivals)
+    own[0].wait()
+    own[1].wait()
 
     def last_arrivals(turn, carry):
         copy(2, turn)[1].wait_recv()
@@ -330,7 +387,7 @@
     per_row = LANES * fitness_class.shape[0] // length
     slab_classes = fitness_class.shape[0] // count
     interleaved = krylov.reshape(vectors, length // LANES, LANES).transpose(1, 0, 2)
-    interleaved = interleaved.reshape(vectors * length // LANES, LANES)
+    interleaved = interleaved.reshape(count, vectors * rows, LANES)
     classes = fitness_class.reshape(count, slab_classes)
     if slab_classes < LANES:
         classes = jnp.pad(classes, ((0, 0), (0, LANES - slab_classes)))
@@ -341,7 +398,7 @@
     landed = pl.pallas_call(
         functools.partial(exchange_kernel, (wide, narrow, rows, local_bits, per_row)),
         out_shape=jax.ShapeDtypeStruct((vectors, count, rows, LANES), f32),
-        in_specs=[vmem, vmem, smem],
+        in_specs=[pl.BlockSpec(memory_space=pl.ANY), vmem, smem],
         out_specs=pl.BlockSpec(memory_space=pl.ANY),
         scratch_shapes=[
             pltpu.VMEM((count, rows + ROWS, LANES), f32),
@@ -355,12 +412,14 @@
             pltpu.VMEM((vectors, LANES, LANES), bf16),
             pltpu.VMEM((vectors, rows, rows), bf16),
             pltpu.VMEM((vectors, rows, rows), bf16),
+            pltpu.VMEM((count, vectors * rows, LANES), f32),
             pltpu.SemaphoreType.DMA((4, count)),
             pltpu.SemaphoreType.DMA((4, count)),
             pltpu.SemaphoreType.DMA((2,)),
+            pltpu.SemaphoreType.DMA((4,)),
         ],
         compiler_params=pltpu.CompilerParams(
-            collective_id=0, has_side_effects=True, vmem_limit_bytes=44 * 1024 * 1024
+            collective_id=0, has_side_effects=True, vmem_limit_bytes=60 * 1024 * 1024
         ),
         name="exchange",
     )(interleaved, classes, rate_index)
@@ -377,7 +436,7 @@
         ],
         out_specs=pl.BlockSpec((count, vectors * block, LANES), lambda step: (0, step, 0)),
         scratch_shapes=[pltpu.VMEM((count, block, LANES), f32)],
-        compiler_params=pltpu.CompilerParams(vmem_limit_bytes=40 * 1024 * 1024),
+        compiler_params=pltpu.CompilerParams(vmem_limit_bytes=60 * 1024 * 1024),
         name="finish",
     )(landed, rate_index)
     mixed = mixed.reshape(length // LANES, vectors, LANES).transpose(1, 0, 2)

time: 206 us -> 201 us (0.976)
  local copies, waits for them, and re-layouts: 3.68 us -> 0 us
    unnamed x6 -> x0, local copies, waits for them, and re-layouts: 3.68 us -> none
    pallas_call x1, Pallas kernels: 198 us -> 195 us  [per_device(): pl.pallas_call(functools.partial(exchange_kernel, (wide, narrow, rows, lo...]
where the time goes in v3:
time: 201 us; the launch traced here: 200 us
  Pallas kernels  200 us (100%)
    pallas_call x1, Pallas kernels, per_device(): pl.pallas_call(functools.partial(exchange_kernel, (wide, narrow, rows, lo...  195 us
    pallas_call x1, Pallas kernels, per_device(): pl.pallas_call(functools.partial(finish_kernel, (device_bits, low_bits),...  5.84 us

profile of v3, /device:TPU:9, one launch (start us, length us, event | category | flops | bytes accessed | tf_op | source)
XLA Modules:
  0.0 200.4 jit_solution(11324225956491738560)
XLA Ops:
  0.0 194.6 %exchange.1.land_ref = f32[2,32,128,128]{3,2,1,0:T(8,128)} custom-call(f32[32,256,128]{2,1,0:T(8,128)} %bitcast.11, s32[32,4,128]{2,1,0:T(4,128)} %bitcast.12, s32[2]{0:T(128)} %rate_ref.3), custom_call_target="tpu_custom_call" | custom-call | tf_op jit(solution)/shard_map/exchange/pallas_call | solution.py:398
  194.6 5.8 %finish.1 = f32[32,256,128]{2,1,0:T(8,128)} custom-call(f32[2,32,128,128]{3,2,1,0:T(8,128)} %exchange.1.land_ref, s32[2]{0:T(128)} %rate_ref.3), custom_call_target="tpu_custom_call" | custom-call | tf_op jit(solution)/shard_map/finish/pallas_call | solution.py:429

commit v4 on v3

--- a/solution.py
+++ b/solution.py
@@ -91,17 +91,10 @@
     lax.fori_loop(0, others * tiles, body, 0)
 
 
-def xor(left, right, bits):
-    both = 0
-    for bit in range(bits):
-        both = both + (1 << bit) * (((left // (1 << bit)) % 2) * ((right // (1 << bit)) % 2))
-    return left + right - 2 * both
-
-
 def exchange_kernel(
-    sizes, x_hbm, class_ref, rate_ref, out_ref,
+    sizes, x_hbm, class_hbm, rate_ref, out_ref,
     send_a, send_b, land_a, land_b, scale_here, scale_moved, back, lane_high, lane_low,
-    mid_high, mid_low, held, send_sem, land_sem, own_sem, load_sem,
+    mid_high, mid_low, held, class_ref, send_sem, land_sem, own_sem, load_sem,
 ):
     wide, narrow, rows, local_bits, per_row = sizes
     count = wide * narrow
@@ -109,19 +102,26 @@
     device_bits = wide_bits + narrow_bits
     low_bits = local_bits - device_bits
     tiles = rows // ROWS
-    class_rows = class_ref.shape[1]
+    class_rows = class_hbm.shape[1]
     profile = profile_of(local_bits + device_bits)
     my_wide, my_narrow = lax.axis_index("wide"), lax.axis_index("narrow")
     me = my_wide * narrow + my_narrow
 
-    def partner(turn):
-        offset = (turn % 2) * (count // 2) + turn // 2
-        to_wide = xor(my_wide, offset // narrow, wide_bits)
-        to_narrow = xor(my_narrow, offset % narrow, narrow_bits)
-        return offset, to_wide, to_narrow, to_wide * narrow + to_narrow
+    flips = [(1 << bit) * (1 - 2 * lax.rem(lax.div(me, 1 << bit), 2)) for bit in range(device_bits)]
+
+    def partners(pair):
+        near = me
+        for bit in range(device_bits - 1):
+            near = near + flips[bit] * lax.rem(lax.div(pair, 1 << bit), 2)
+        return (pair, near), (pair + count // 2, near + flips[-1])
+
+    def place(flat):
+        return (lax.div(flat, narrow), lax.rem(flat, narrow))
 
     chunks = min(4, tiles)
     chunk_rows = 2 * rows // chunks
+    class_load = pltpu.make_async_copy(class_hbm, class_ref, load_sem.at[chunks])
+    class_load.start()
     loads = []
     for chunk in range(chunks):
         part = pl.ds(chunk * chunk_rows, chunk_rows)
@@ -132,26 +132,37 @@
 
     barrier = pltpu.get_barrier_semaphore()
 
-    def greet(turn, carry):
-        _, to_wide, to_narrow, _ = partner(turn)
-        pl.semaphore_signal(
-            barrier, inc=1, device_id=(to_wide, to_narrow), device_id_type=pl.DeviceIdType.MESH
-        )
-        return carry
-
-    lax.fori_loop(1, count, greet, 0)
+    def each_pair(step):
+        step(*partners(0), True)
+
+        def body(pair, carry):
+            step(*partners(pair), False)
+            return carry
+
+        lax.fori_loop(1, count // 2, body, 0)
+
+    def sent(near, far, own):
+        return [far] if own else [far, near]
+
+    def greet(near, far, own):
+        for _, flat in sent(near, far, own):
+            pl.semaphore_signal(
+                barrier, inc=1, device_id=place(flat), device_id_type=pl.DeviceIdType.MESH
+            )
+
+    each_pair(greet)
 
     def copy(stage, turn):
-        offset, to_wide, to_narrow, flat = partner(turn)
+        offset, flat = turn
         source, target = (
             (send_a, land_a), (send_b, land_b), (back.at[0], out_ref.at[0]), (back.at[1], out_ref.at[1])
         )[stage]
-        return flat, pltpu.make_async_remote_copy(
+        return pltpu.make_async_remote_copy(
             src_ref=source.at[flat],
             dst_ref=target.at[me],
             send_sem=send_sem.at[stage, offset],
             recv_sem=land_sem.at[stage, offset],
-            device_id=(to_wide, to_narrow),
+            device_id=place(flat),
             device_id_type=pl.DeviceIdType.MESH,
         )
 
@@ -189,15 +200,14 @@
         for member in range(together):
             at = step * together + member
             compact = 0.5 + 0.25 * class_ref[at].astype(jnp.float32)
-            send_a[at, rows:, :] = jnp.concatenate(
-                [compact, jnp.zeros((ROWS - class_rows, LANES), jnp.float32)], axis=0
-            )
+            send_a[at, rows:, :] = compact
             compacts.append(compact)
         spread = expand(compacts)
         for member in range(together):
             scale_here[step * together + member] = spread[member * rows : (member + 1) * rows]
         return carry
 
+    class_load.wait()
     lax.fori_loop(0, count // together, spread_here, 0)
 
     def tile_rows(tile):
@@ -254,46 +264,31 @@
         for group in groups[:-1]:
             group_pass(group, device_bits, tiles, rates, load, store)
 
-    def each_pair(step):
-        step(0, True)
-
-        def body(pair, carry):
-            step(pair, False)
-            return carry
-
-        lax.fori_loop(1, count // 2, body, 0)
-
-    def turns_of(pair, with_own):
-        return [2 * pair + 1] if with_own else [2 * pair, 2 * pair + 1]
-
-    def slabs_of(pair):
-        return [partner(2 * pair)[3], partner(2 * pair + 1)[3]]
-
     for chunk in range(chunks):
         loads[chunk].wait()
         prepare(0, send_a, chunk)
     pl.semaphore_wait(barrier, count - 1)
 
-    def start_first(turn, carry):
-        copy(0, turn)[1].start()
-        return carry
-
-    lax.fori_loop(1, count, start_first, 0)
+    def start_first(near, far, own):
+        for turn in sent(near, far, own):
+            copy(0, turn).start()
+
+    each_pair(start_first)
     build_matrices()
     for chunk in range(chunks):
         prepare(1, send_b, chunk)
 
-    def first_arrivals(pair, with_own):
-        turns = turns_of(pair, with_own)
+    def first_arrivals(near, far, own):
+        turns = sent(near, far, own)
         for turn in turns:
-            copy(0, turn)[1].wait_send()
-            copy(1, turn)[1].start()
+            copy(0, turn).wait_send()
+            copy(1, turn).start()
         for turn in turns:
-            copy(0, turn)[1].wait_recv()
-        slabs = slabs_of(pair)
-        sources = [send_a if with_own and not at else land_a for at in range(2)]
+            copy(0, turn).wait_recv()
+        slabs = [near[1], far[1]]
+        sources = [send_a if own else land_a, land_a]
         mixed = low_mix([source[flat, :rows, :] for source, flat in zip(sources, slabs)], 0)
-        spread = expand([source[flat, rows : rows + class_rows, :] for source, flat in zip(sources, slabs)])
+        spread = expand([source[flat, rows:, :] for source, flat in zip(sources, slabs)])
         for at, flat in enumerate(slabs):
             land_a[flat, :rows, :] = mixed[at]
             scale_moved[flat] = spread[at * rows : (at + 1) * rows]
@@ -301,28 +296,28 @@
     each_pair(first_arrivals)
     turn_over(0, land_a)
 
-    own = [
+    kept = [
         pltpu.make_async_copy(back.at[vector, me], out_ref.at[vector, me], own_sem.at[vector])
         for vector in range(2)
     ]
 
-    def send_back(vector, landed, pair, with_own):
-        slabs = slabs_of(pair)
+    def send_back(vector, landed, near, far, own):
+        slabs = [near[1], far[1]]
         mixed = low_mix([landed[flat, :rows, :] for flat in slabs], vector)
         for flat, values in zip(slabs, mixed):
             back[vector, flat] = values
-        if with_own:
-            own[vector].start()
-        for turn in turns_of(pair, with_own):
-            copy(1 + vector, turn)[1].wait_send()
-            copy(2 + vector, turn)[1].start()
-
-    def second_arrivals(pair, with_own):
-        send_back(0, land_a, pair, with_own)
-        for turn in turns_of(pair, with_own):
-            copy(1, turn)[1].wait_recv()
-        slabs = slabs_of(pair)
-        sources = [send_b if with_own and not at else land_b for at in range(2)]
+        if own:
+            kept[vector].start()
+        for turn in sent(near, far, own):
+            copy(1 + vector, turn).wait_send()
+            copy(2 + vector, turn).start()
+
+    def second_arrivals(near, far, own):
+        send_back(0, land_a, near, far, own)
+        for turn in sent(near, far, own):
+            copy(1, turn).wait_recv()
+        slabs = [near[1], far[1]]
+        sources = [send_b if own else land_b, land_b]
         mixed = low_mix([source[flat] for source, flat in zip(sources, slabs)], 1)
         for flat, values in zip(slabs, mixed):
             land_b[flat] = values
@@ -330,19 +325,19 @@
     each_pair(second_arrivals)
     turn_over(1, land_b)
 
-    def third_arrivals(pair, with_own):
-        send_back(1, land_b, pair, with_own)
+    def third_arrivals(near, far, own):
+        send_back(1, land_b, near, far, own)
 
     each_pair(third_arrivals)
-    own[0].wait()
-    own[1].wait()
-
-    def last_arrivals(turn, carry):
-        copy(2, turn)[1].wait_recv()
-        copy(3, turn)[1].wait()
-        return carry
-
-    lax.fori_loop(1, count, last_arrivals, 0)
+    kept[0].wait()
+    kept[1].wait()
+
+    def last_arrivals(near, far, own):
+        for turn in sent(near, far, own):
+            copy(2, turn).wait_recv()
+            copy(3, turn).wait()
+
+    each_pair(last_arrivals)
 
 
 def finish_kernel(sizes, profile, land_ref, rate_ref, out_ref, held):
@@ -393,17 +388,16 @@
         classes = jnp.pad(classes, ((0, 0), (0, LANES - slab_classes)))
     classes = classes.reshape(count, -1, LANES)
     f32, bf16 = jnp.float32, jnp.bfloat16
-    vmem = pl.BlockSpec(memory_space=pltpu.VMEM)
     smem = pl.BlockSpec(memory_space=pltpu.SMEM)
     landed = pl.pallas_call(
         functools.partial(exchange_kernel, (wide, narrow, rows, local_bits, per_row)),
         out_shape=jax.ShapeDtypeStruct((vectors, count, rows, LANES), f32),
-        in_specs=[pl.BlockSpec(memory_space=pl.ANY), vmem, smem],
+        in_specs=[pl.BlockSpec(memory_space=pl.ANY), pl.BlockSpec(memory_space=pl.ANY), smem],
         out_specs=pl.BlockSpec(memory_space=pl.ANY),
         scratch_shapes=[
-            pltpu.VMEM((count, rows + ROWS, LANES), f32),
+            pltpu.VMEM((count, rows + classes.shape[1], LANES), f32),
             pltpu.VMEM((count, rows, LANES), f32),
-            pltpu.VMEM((count, rows + ROWS, LANES), f32),
+            pltpu.VMEM((count, rows + classes.shape[1], LANES), f32),
             pltpu.VMEM((count, rows, LANES), f32),
             pltpu.VMEM((count, rows, LANES), f32),
             pltpu.VMEM((count, rows, LANES), f32),
@@ -413,10 +407,11 @@
             pltpu.VMEM((vectors, rows, rows), bf16),
             pltpu.VMEM((vectors, rows, rows), bf16),
             pltpu.VMEM((count, vectors * rows, LANES), f32),
+            pltpu.VMEM(classes.shape, jnp.int32),
             pltpu.SemaphoreType.DMA((4, count)),
             pltpu.SemaphoreType.DMA((4, count)),
             pltpu.SemaphoreType.DMA((2,)),
-            pltpu.SemaphoreType.DMA((4,)),
+            pltpu.SemaphoreType.DMA((5,)),
         ],
         compiler_params=pltpu.CompilerParams(
             collective_id=0, has_side_effects=True, vmem_limit_bytes=60 * 1024 * 1024

time: 201 us -> 198 us (0.985)
    pallas_call x1, Pallas kernels: 195 us -> 192 us  [per_device(): pl.pallas_call(functools.partial(exchange_kernel, (wide, narrow, rows, lo...]
where the time goes in v4:
time: 198 us
  Pallas kernels  198 us (100%)
    pallas_call x1, Pallas kernels, per_device(): pl.pallas_call(functools.partial(exchange_kernel, (wide, narrow, rows, lo...  192 us
    pallas_call x1, Pallas kernels, per_device(): pl.pallas_call(functools.partial(finish_kernel, (device_bits, low_bits),...  5.84 us

profile of v4, /device:TPU:9, one launch (start us, length us, event | category | flops | bytes accessed | tf_op | source)
XLA Modules:
  0.0 197.6 jit_solution(9911718970487088715)
XLA Ops:
  0.0 191.7 %exchange.1.land_ref = f32[2,32,128,128]{3,2,1,0:T(8,128)} custom-call(f32[32,256,128]{2,1,0:T(8,128)} %bitcast.11, s32[32,4,128]{2,1,0:T(4,128)} %bitcast.12, s32[2]{0:T(128)} %rate_ref.3), custom_call_target="tpu_custom_call" | custom-call | tf_op jit(solution)/shard_map/exchange/pallas_call | solution.py:392
  191.7 5.8 %finish.1 = f32[32,256,128]{2,1,0:T(8,128)} custom-call(f32[2,32,128,128]{3,2,1,0:T(8,128)} %exchange.1.land_ref, s32[2]{0:T(128)} %rate_ref.3), custom_call_target="tpu_custom_call" | custom-call | tf_op jit(solution)/shard_map/finish/pallas_call | solution.py:424

commit v5 on v4

--- a/solution.py
+++ b/solution.py
@@ -94,7 +94,7 @@
 def exchange_kernel(
     sizes, x_hbm, class_hbm, rate_ref, out_ref,
     send_a, send_b, land_a, land_b, scale_here, scale_moved, back, lane_high, lane_low,
-    mid_high, mid_low, held, class_ref, send_sem, land_sem, own_sem, load_sem,
+    mid_high, mid_low, held, class_ref, land_c, send_sem, land_sem, own_sem, load_sem,
 ):
     wide, narrow, rows, local_bits, per_row = sizes
     count = wide * narrow
@@ -112,7 +112,7 @@
     def partners(pair):
         near = me
         for bit in range(device_bits - 1):
-            near = near + flips[bit] * lax.rem(lax.div(pair, 1 << bit), 2)
+            near = near + flips[device_bits - 2 - bit] * lax.rem(lax.div(pair, 1 << bit), 2)
         return (pair, near), (pair + count // 2, near + flips[-1])
 
     def place(flat):
@@ -155,7 +155,7 @@
     def copy(stage, turn):
         offset, flat = turn
         source, target = (
-            (send_a, land_a), (send_b, land_b), (back.at[0], out_ref.at[0]), (back.at[1], out_ref.at[1])
+            (send_a, land_a), (send_b, land_b), (back.at[0], land_c), (back.at[1], out_ref.at[1])
         )[stage]
         return pltpu.make_async_remote_copy(
             src_ref=source.at[flat],
@@ -296,18 +296,18 @@
     each_pair(first_arrivals)
     turn_over(0, land_a)
 
-    kept = [
-        pltpu.make_async_copy(back.at[vector, me], out_ref.at[vector, me], own_sem.at[vector])
-        for vector in range(2)
-    ]
+    own_copy = pltpu.make_async_copy(back.at[1, me], out_ref.at[1, me], own_sem.at[0])
 
     def send_back(vector, landed, near, far, own):
         slabs = [near[1], far[1]]
         mixed = low_mix([landed[flat, :rows, :] for flat in slabs], vector)
-        for flat, values in zip(slabs, mixed):
-            back[vector, flat] = values
-        if own:
-            kept[vector].start()
+        if own and vector == 0:
+            land_c[me] = mixed[0]
+        else:
+            back[vector, slabs[0]] = mixed[0]
+        back[vector, slabs[1]] = mixed[1]
+        if own and vector == 1:
+            own_copy.start()
         for turn in sent(near, far, own):
             copy(1 + vector, turn).wait_send()
             copy(2 + vector, turn).start()
@@ -329,15 +329,28 @@
         send_back(1, land_b, near, far, own)
 
     each_pair(third_arrivals)
-    kept[0].wait()
-    kept[1].wait()
+    def third_landed(near, far, own):
+        for turn in sent(near, far, own):
+            copy(2, turn).wait_recv()
+
+    each_pair(third_landed)
+    rates = rates_of(rate_ref, 0, profile, low_bits, device_bits)
+    for group in groups_of(device_bits):
+        group_pass(
+            group, device_bits, tiles, rates,
+            lambda at, tile: land_c[at, tile_rows(tile), :],
+            lambda at, tile, value: land_c.__setitem__((at, tile_rows(tile), slice(None)), value),
+        )
+    first_out = pltpu.make_async_copy(land_c, out_ref.at[0], own_sem.at[1])
+    first_out.start()
+    own_copy.wait()
 
     def last_arrivals(near, far, own):
         for turn in sent(near, far, own):
-            copy(2, turn).wait_recv()
             copy(3, turn).wait()
 
     each_pair(last_arrivals)
+    first_out.wait()
 
 
 def finish_kernel(sizes, profile, land_ref, rate_ref, out_ref, held):
@@ -348,27 +361,29 @@
     def tile_rows(tile):
         return pl.ds(pl.multiple_of(tile * ROWS, ROWS), ROWS)
 
-    for vector in range(2):
-        rates = rates_of(rate_ref, vector, profile, low_bits, device_bits)
-
-        def first_load(at, tile):
-            return land_ref[vector, at, tile_rows(tile), :]
-
-        def load(at, tile):
-            return held[at, tile_rows(tile), :]
-
+    def landed(vector):
+        return lambda at, tile: land_ref[vector, at, tile_rows(tile), :]
+
+    def final(vector):
         def store(at, tile, value):
-            held[at, tile_rows(tile), :] = value
-
-        def last_store(at, tile, value):
             out_ref[at, pl.ds(2 * ROWS * tile + vector, ROWS, stride=2), :] = value
 
-        for number, group in enumerate(groups):
-            group_pass(
-                group, device_bits, tiles, rates,
-                load if number else first_load,
-                last_store if number == len(groups) - 1 else store,
-            )
+        return store
+
+    def load(at, tile):
+        return held[at, tile_rows(tile), :]
+
+    def store(at, tile, value):
+        held[at, tile_rows(tile), :] = value
+
+    group_pass(groups[0], device_bits, tiles, [], landed(0), final(0))
+    rates = rates_of(rate_ref, 1, profile, low_bits, device_bits)
+    for number, group in enumerate(groups):
+        group_pass(
+            group, device_bits, tiles, rates,
+            load if number else landed(1),
+            final(1) if number == len(groups) - 1 else store,
+        )
 
 
 def per_device(krylov, fitness_class, rate_index):
@@ -408,6 +423,7 @@
             pltpu.VMEM((vectors, rows, rows), bf16),
             pltpu.VMEM((count, vectors * rows, LANES), f32),
             pltpu.VMEM(classes.shape, jnp.int32),
+            pltpu.VMEM((count, rows, LANES), f32),
             pltpu.SemaphoreType.DMA((4, count)),
             pltpu.SemaphoreType.DMA((4, count)),
             pltpu.SemaphoreType.DMA((2,)),

time: 198 us -> 199 us (level)
  no operation moved by 1% of the time
where the time goes in v5:
time: 199 us; the launch traced here: 198 us
  Pallas kernels  198 us (99%)
    pallas_call x1, Pallas kernels, per_device(): pl.pallas_call(functools.partial(exchange_kernel, (wide, narrow, rows, lo...  192 us
    pallas_call x1, Pallas kernels, per_device(): pl.pallas_call(functools.partial(finish_kernel, (device_bits, low_bits),...  5.37 us

profile of v5, /device:TPU:9, one launch (start us, length us, event | category | flops | bytes accessed | tf_op | source)
XLA Modules:
  0.0 197.8 jit_solution(2147894561080955107)
XLA Ops:
  0.0 192.4 %exchange.1.land_ref = f32[2,32,128,128]{3,2,1,0:T(8,128)} custom-call(f32[32,256,128]{2,1,0:T(8,128)} %bitcast.11, s32[32,4,128]{2,1,0:T(4,128)} %bitcast.12, s32[2]{0:T(128)} %rate_ref.3), custom_call_target="tpu_custom_call" | custom-call | tf_op jit(solution)/shard_map/exchange/pallas_call | solution.py:407
  192.4 5.4 %finish.1 = f32[32,256,128]{2,1,0:T(8,128)} custom-call(f32[2,32,128,128]{3,2,1,0:T(8,128)} %exchange.1.land_ref, s32[2]{0:T(128)} %rate_ref.3), custom_call_target="tpu_custom_call" | custom-call | tf_op jit(solution)/shard_map/finish/pallas_call | solution.py:440

commit v6 on v5

--- a/solution.py
+++ b/solution.py
@@ -109,11 +109,12 @@
 
     flips = [(1 << bit) * (1 - 2 * lax.rem(lax.div(me, 1 << bit), 2)) for bit in range(device_bits)]
 
-    def partners(pair):
-        near = me
-        for bit in range(device_bits - 1):
-            near = near + flips[device_bits - 2 - bit] * lax.rem(lax.div(pair, 1 << bit), 2)
-        return (pair, near), (pair + count // 2, near + flips[-1])
+    def partners(pair, far):
+        first = me + flips[-1] if far else me
+        for bit in range(1, device_bits - 1):
+            first = first + flips[bit] * lax.rem(lax.div(pair, 1 << (bit - 1)), 2)
+        offset = 2 * pair + (count // 2 if far else 0)
+        return (offset, first), (offset + 1, first + flips[0])
 
     def place(flat):
         return (lax.div(flat, narrow), lax.rem(flat, narrow))
@@ -133,19 +134,23 @@
     barrier = pltpu.get_barrier_semaphore()
 
     def each_pair(step):
-        step(*partners(0), True)
-
-        def body(pair, carry):
-            step(*partners(pair), False)
+        def far_body(pair, carry):
+            step(*partners(pair, True), False)
             return carry
 
-        lax.fori_loop(1, count // 2, body, 0)
-
-    def sent(near, far, own):
-        return [far] if own else [far, near]
-
-    def greet(near, far, own):
-        for _, flat in sent(near, far, own):
+        def near_body(pair, carry):
+            step(*partners(pair, False), False)
+            return carry
+
+        lax.fori_loop(0, count // 4, far_body, 0)
+        step(*partners(0, False), True)
+        lax.fori_loop(1, count // 4, near_body, 0)
+
+    def sent(first, second, own):
+        return [second] if own else [first, second]
+
+    def greet(first, second, own):
+        for _, flat in sent(first, second, own):
             pl.semaphore_signal(
                 barrier, inc=1, device_id=place(flat), device_id_type=pl.DeviceIdType.MESH
             )
@@ -269,8 +274,8 @@
         prepare(0, send_a, chunk)
     pl.semaphore_wait(barrier, count - 1)
 
-    def start_first(near, far, own):
-        for turn in sent(near, far, own):
+    def start_first(first, second, own):
+        for turn in sent(first, second, own):
             copy(0, turn).start()
 
     each_pair(start_first)
@@ -278,14 +283,14 @@
     for chunk in range(chunks):
         prepare(1, send_b, chunk)
 
-    def first_arrivals(near, far, own):
-        turns = sent(near, far, own)
+    def first_arrivals(first, second, own):
+        turns = sent(first, second, own)
         for turn in turns:
             copy(0, turn).wait_send()
             copy(1, turn).start()
         for turn in turns:
             copy(0, turn).wait_recv()
-        slabs = [near[1], far[1]]
+        slabs = [first[1], second[1]]
         sources = [send_a if own else land_a, land_a]
         mixed = low_mix([source[flat, :rows, :] for source, flat in zip(sources, slabs)], 0)
         spread = expand([source[flat, rows:, :] for source, flat in zip(sources, slabs)])
@@ -298,8 +303,8 @@
 
     own_copy = pltpu.make_async_copy(back.at[1, me], out_ref.at[1, me], own_sem.at[0])
 
-    def send_back(vector, landed, near, far, own):
-        slabs = [near[1], far[1]]
+    def send_back(vector, landed, first, second, own):
+        slabs = [first[1], second[1]]
         mixed = low_mix([landed[flat, :rows, :] for flat in slabs], vector)
         if own and vector == 0:
             land_c[me] = mixed[0]
@@ -308,15 +313,15 @@
         back[vector, slabs[1]] = mixed[1]
         if own and vector == 1:
             own_copy.start()
-        for turn in sent(near, far, own):
+        for turn in sent(first, second, own):
             copy(1 + vector, turn).wait_send()
             copy(2 + vector, turn).start()
 
-    def second_arrivals(near, far, own):
-        send_back(0, land_a, near, far, own)
-        for turn in sent(near, far, own):
+    def second_arrivals(first, second, own):
+        send_back(0, land_a, first, second, own)
+        for turn in sent(first, second, own):
             copy(1, turn).wait_recv()
-        slabs = [near[1], far[1]]
+        slabs = [first[1], second[1]]
         sources = [send_b if own else land_b, land_b]
         mixed = low_mix([source[flat] for source, flat in zip(sources, slabs)], 1)
         for flat, values in zip(slabs, mixed):
@@ -325,12 +330,12 @@
     each_pair(second_arrivals)
     turn_over(1, land_b)
 
-    def third_arrivals(near, far, own):
-        send_back(1, land_b, near, far, own)
+    def third_arrivals(first, second, own):
+        send_back(1, land_b, first, second, own)
 
     each_pair(third_arrivals)
-    def third_landed(near, far, own):
-        for turn in sent(near, far, own):
+    def third_landed(first, second, own):
+        for turn in sent(first, second, own):
             copy(2, turn).wait_recv()
 
     each_pair(third_landed)
@@ -345,8 +350,8 @@
     first_out.start()
     own_copy.wait()
 
-    def last_arrivals(near, far, own):
-        for turn in sent(near, far, own):
+    def last_arrivals(first, second, own):
+        for turn in sent(first, second, own):
             copy(3, turn).wait()
 
     each_pair(last_arrivals)
@@ -435,7 +440,7 @@
         name="exchange",
     )(interleaved, classes, rate_index)
 
-    block = min(rows, 32)
+    block = min(rows, 16)
     profile = profile_of(local_bits + device_bits)
     mixed = pl.pallas_call(
         functools.partial(finish_kernel, (device_bits, low_bits), profile),

time: 199 us -> 206 us (1.035)
  Pallas kernels: 198 us -> 204 us
    pallas_call x1, Pallas kernels: 192 us -> 197 us  [per_device(): pl.pallas_call(functools.partial(exchange_kernel, (wide, narrow, rows, lo...]
where the time goes in v6:
time: 206 us; the launch traced here: 204 us
  Pallas kernels  204 us (99%)
    pallas_call x1, Pallas kernels, per_device(): pl.pallas_call(functools.partial(exchange_kernel, (wide, narrow, rows, lo...  197 us
    pallas_call x1, Pallas kernels, per_device(): pl.pallas_call(functools.partial(finish_kernel, (device_bits, low_bits),...  7.16 us

profile of v6, /device:TPU:9, one launch (start us, length us, event | category | flops | bytes accessed | tf_op | source)
XLA Modules:
  0.0 203.9 jit_solution(8345085672887866960)
XLA Ops:
  0.0 196.7 %exchange.1.land_ref = f32[2,32,128,128]{3,2,1,0:T(8,128)} custom-call(f32[32,256,128]{2,1,0:T(8,128)} %bitcast.11, s32[32,4,128]{2,1,0:T(4,128)} %bitcast.12, s32[2]{0:T(128)} %rate_ref.3), custom_call_target="tpu_custom_call" | custom-call | tf_op jit(solution)/shard_map/exchange/pallas_call | solution.py:412
  196.7 7.2 %finish.1 = f32[32,256,128]{2,1,0:T(8,128)} custom-call(f32[2,32,128,128]{3,2,1,0:T(8,128)} %exchange.1.land_ref, s32[2]{0:T(128)} %rate_ref.3), custom_call_target="tpu_custom_call" | custom-call | tf_op jit(solution)/shard_map/finish/pallas_call | solution.py:445

commit v7 on v5

--- a/solution.py
+++ b/solution.py
@@ -112,7 +112,7 @@
     def partners(pair):
         near = me
         for bit in range(device_bits - 1):
-            near = near + flips[device_bits - 2 - bit] * lax.rem(lax.div(pair, 1 << bit), 2)
+            near = near + flips[bit] * lax.rem(lax.div(pair, 1 << bit), 2)
         return (pair, near), (pair + count // 2, near + flips[-1])
 
     def place(flat):
@@ -435,7 +435,7 @@
         name="exchange",
     )(interleaved, classes, rate_index)
 
-    block = min(rows, 32)
+    block = min(rows, 64)
     profile = profile_of(local_bits + device_bits)
     mixed = pl.pallas_call(
         functools.partial(finish_kernel, (device_bits, low_bits), profile),

time: 199 us -> 196 us (0.985)
  Pallas kernels: 198 us -> 196 us
where the time goes in v7:
time: 196 us
  Pallas kernels  196 us (100%)
    pallas_call x1, Pallas kernels, per_device(): pl.pallas_call(functools.partial(exchange_kernel, (wide, narrow, rows, lo...  192 us
    pallas_call x1, Pallas kernels, per_device(): pl.pallas_call(functools.partial(finish_kernel, (device_bits, low_bits),...  4.43 us

profile of v7, /device:TPU:9, one launch (start us, length us, event | category | flops | bytes accessed | tf_op | source)
XLA Modules:
  0.0 196.2 jit_solution(8106812801438832985)
XLA Ops:
  0.0 191.7 %exchange.1.land_ref = f32[2,32,128,128]{3,2,1,0:T(8,128)} custom-call(f32[32,256,128]{2,1,0:T(8,128)} %bitcast.11, s32[32,4,128]{2,1,0:T(4,128)} %bitcast.12, s32[2]{0:T(128)} %rate_ref.3), custom_call_target="tpu_custom_call" | custom-call | tf_op jit(solution)/shard_map/exchange/pallas_call | solution.py:407
  191.7 4.4 %finish.1 = f32[32,256,128]{2,1,0:T(8,128)} custom-call(f32[2,32,128,128]{3,2,1,0:T(8,128)} %exchange.1.land_ref, s32[2]{0:T(128)} %rate_ref.3), custom_call_target="tpu_custom_call" | custom-call | tf_op jit(solution)/shard_map/finish/pallas_call | solution.py:440

commit v8 on v7

--- a/solution.py
+++ b/solution.py
@@ -136,7 +136,7 @@
         step(*partners(0), True)
 
         def body(pair, carry):
-            step(*partners(pair), False)
+            step(*partners(count // 2 - pair), False)
             return carry
 
         lax.fori_loop(1, count // 2, body, 0)

time: 196 us -> 199 us (1.015)
  the two profiles are of different devices: /device:TPU:9 before, /device:TPU:0 now
where the time goes in v8:
time: 199 us
  Pallas kernels  199 us (100%)
    pallas_call x1, Pallas kernels, per_device(): pl.pallas_call(functools.partial(exchange_kernel, (wide, narrow, rows, lo...  194 us
    pallas_call x1, Pallas kernels, per_device(): pl.pallas_call(functools.partial(finish_kernel, (device_bits, low_bits),...  4.43 us

profile of v8, /device:TPU:0, one launch (start us, length us, event | category | flops | bytes accessed | tf_op | source)
XLA Modules:
  0.0 198.7 jit_solution(6631633551740283297)
XLA Ops:
  0.0 194.3 %exchange.1.land_ref = f32[2,32,128,128]{3,2,1,0:T(8,128)} custom-call(f32[32,256,128]{2,1,0:T(8,128)} %bitcast.11, s32[32,4,128]{2,1,0:T(4,128)} %bitcast.12, s32[2]{0:T(128)} %rate_ref.3), custom_call_target="tpu_custom_call" | custom-call | tf_op jit(solution)/shard_map/exchange/pallas_call | solution.py:407
  194.3 4.4 %finish.1 = f32[32,256,128]{2,1,0:T(8,128)} custom-call(f32[2,32,128,128]{3,2,1,0:T(8,128)} %exchange.1.land_ref, s32[2]{0:T(128)} %rate_ref.3), custom_call_target="tpu_custom_call" | custom-call | tf_op jit(solution)/shard_map/finish/pallas_call | solution.py:440
